TPU v7x, 32 devices: a whole 2x2x4 slice. The times are simulated.
32 devices in a mesh: groups: 2 (over x), view: 16 (over z, y, core).
Axes of the slice: x: 2, y: 2, z: 4, core: 2. Of those that a mesh axis runs over, the one named last changes fastest.
Arguments:
- query_vectors: bfloat16 [32, 16, 8, 4096], P(('groups', 'view')), parts along dimension 0, may hold values from -6 to 6
- key_vectors: bfloat16 [32, 16, 8, 4096], P(('groups', 'view')), parts along dimension 0, may hold values from -6 to 6
- value_vectors: bfloat16 [32, 16, 8, 4096], P(('groups', 'view')), parts along dimension 0, may hold values from -6 to 6
- request_of_slot: int32 [8], P('groups'), parts along dimension 0, may hold values from 0 to 2, as said below
Outputs:
- attended: bfloat16 [32, 16, 8, 4096], P(('groups', 'view')), parts along dimension 0
There are 2 independent parts, one for each index of `groups`. A program takes and returns all parts, laid end to end along the dimension named above; each array names one. Nothing has to cross between parts.
Inputs may be any that keep to these rules, and one draw needn't show every extreme that they name: `request_of_slot`: each request holds 1 to 2 slots, not necessarily consecutive, and one holds exactly 2.
All inputs are finite; a program needn't handle non-finite values.
Results may differ from a plain program's by a relative error of at most 0.0044.
Values may be sent and summed in bfloat16 or wider, within the bound.
A program may use at most 64 MiB of HBM per device.

v0:
```python
import jax
import jax.numpy as jnp
from jax import lax
from jax.experimental import pallas as pl
from jax.experimental.pallas import tpu as pltpu
from jax.sharding import PartitionSpec as P

HEADS = 32
HS = 128
ROWS = 16
COLS = 8
LOG2E = 1.4426950408889634
VMEM_LIMIT = 209 * 256 * 1024


NEG_FILL = -1e30


def partner(value, axis, distance):
    return lax.ppermute(value, axis, [(i, i ^ 1 << distance) for i in range(lax.axis_size(axis))])


def masked_softmax(scores, allowed):
    scores = jnp.where(allowed, scores, NEG_FILL)
    maximum = jnp.max(scores, axis=-1)
    raised = jnp.exp(scores - maximum[..., None])
    totals = jnp.sum(raised, axis=-1)
    return (maximum, totals, raised.astype(jnp.bfloat16))


def combine(first_part, second_part):
    highest = jnp.maximum(first_part[0], second_part[0])
    first_scale = jnp.exp(first_part[0] - highest)
    second_scale = jnp.exp(second_part[0] - highest)
    denominator = first_part[1] * first_scale + second_part[1] * second_scale
    numerator = first_part[2] * first_scale[..., None] + second_part[2] * second_scale[..., None]
    return (numerator / denominator[..., None]).astype(jnp.bfloat16)


def into_rows(tensor, row_blocks, head_groups):
    trailing = tensor.shape[3:]
    block_rows = tensor.shape[0] // row_blocks
    width_cols = tensor.shape[1]
    group_heads = tensor.shape[2] // head_groups
    shaped = tensor.reshape(
        (row_blocks, block_rows, width_cols, head_groups, group_heads) + trailing
    )
    permuted = (0, 3, 1, 2, 4) + tuple(range(5, 5 + len(trailing)))
    return shaped.transpose(permuted).reshape(
        (row_blocks * head_groups, block_rows, width_cols, group_heads) + trailing
    )


def into_tokens(tensor, row_blocks, head_groups):
    trailing = tensor.shape[4:]
    block_rows = tensor.shape[1]
    width_cols = tensor.shape[2]
    group_heads = tensor.shape[3]
    shaped = tensor.reshape(
        (row_blocks, head_groups, block_rows, width_cols, group_heads) + trailing
    )
    permuted = (0, 2, 3, 1, 4) + tuple(range(5, 5 + len(trailing)))
    return shaped.transpose(permuted).reshape(
        (row_blocks * block_rows * width_cols, head_groups * group_heads) + trailing
    )


def general_shards(query_vectors, key_vectors, value_vectors, request_of_slot):
    scaling = HS ** (-0.5)
    token_count = ROWS * COLS
    partner_key, partner_value = partner((key_vectors, value_vectors), "view", 0)
    head_blocks = 4
    block_heads = HEADS // head_blocks
    own_query = query_vectors.reshape(token_count, head_blocks, block_heads, HS)
    both_keys = jnp.concatenate(
        [
            key_vectors.reshape(token_count, head_blocks, block_heads, HS),
            partner_key.reshape(token_count, head_blocks, block_heads, HS),
        ],
        axis=0,
    )
    both_values = jnp.concatenate(
        [
            value_vectors.reshape(token_count, head_blocks, block_heads, HS),
            partner_value.reshape(token_count, head_blocks, block_heads, HS),
        ],
        axis=0,
    )
    query_row = jnp.arange(token_count) // COLS
    key_row = jnp.arange(2 * token_count) % token_count // COLS
    local_allowed = query_row[:, None] != key_row[None, :]

    def local_block(triple):
        block_scores = (
            jnp.einsum("nhx,khx->hnk", triple[0], triple[1], preferred_element_type=jnp.float32)
            * scaling
        )
        block_peak, block_total, block_weights = masked_softmax(block_scores, local_allowed[None])
        block_sum = jnp.einsum(
            "hnk,khx->nhx", block_weights, triple[2], preferred_element_type=jnp.float32
        )
        return (block_peak.T, block_total.T, block_sum)

    block_peaks, block_totals, block_sums = lax.map(
        local_block,
        (
            jnp.moveaxis(own_query, 1, 0),
            jnp.moveaxis(both_keys, 1, 0),
            jnp.moveaxis(both_values, 1, 0),
        ),
    )
    local_peak = jnp.moveaxis(block_peaks, 0, 1).reshape(token_count, HEADS)
    local_total = jnp.moveaxis(block_totals, 0, 1).reshape(token_count, HEADS)
    local_sum = jnp.moveaxis(block_sums, 0, 1).reshape(token_count, HEADS, HS)
    device_count = lax.axis_size("view")
    slot_count = device_count // 4
    pass_images = device_count // 2
    head_groups = 8
    row_blocks = device_count // head_groups
    block_rows = ROWS // row_blocks
    slot_request = jnp.broadcast_to(
        request_of_slot[:, None], (request_of_slot.shape[0], 2 * COLS)
    ).reshape(-1)
    row_allowed = slot_request[:, None] == slot_request[None, :]

    def arrange(tensor):
        shaped = tensor.reshape(slot_count, 2, 2, block_rows, COLS, HS).transpose(1, 3, 0, 2, 4, 5)
        return shaped.reshape(2 * block_rows, pass_images * COLS, HS)

    def restore(tensor):
        trailing = tensor.shape[2:]
        shaped = tensor.reshape((2, block_rows, slot_count, 2, COLS) + trailing)
        permuted = (2, 0, 3, 1, 4) + tuple(range(5, 5 + len(trailing)))
        return shaped.transpose(permuted).reshape((device_count, block_rows, COLS) + trailing)

    def one_head(triple):
        row_scores = (
            jnp.einsum(
                "bnx,bkx->bnk",
                arrange(triple[0]),
                arrange(triple[1]),
                preferred_element_type=jnp.float32,
            )
            * scaling
        )
        row_peak, row_total, row_weights = masked_softmax(row_scores, row_allowed[None])
        row_sum = jnp.einsum(
            "bnk,bkx->bnx", row_weights, arrange(triple[2]), preferred_element_type=jnp.float32
        )
        return (restore(row_peak), restore(row_total), restore(row_sum))

    query_rows = into_rows(query_vectors.reshape(ROWS, COLS, HEADS, HS), row_blocks, head_groups)
    key_rows = into_rows(key_vectors.reshape(ROWS, COLS, HEADS, HS), row_blocks, head_groups)
    value_rows = into_rows(value_vectors.reshape(ROWS, COLS, HEADS, HS), row_blocks, head_groups)
    by_head = (
        jnp.moveaxis(
            lax.all_to_all(query_rows, "view", split_axis=0, concat_axis=0, tiled=True), 3, 0
        ),
        jnp.moveaxis(
            lax.all_to_all(key_rows, "view", split_axis=0, concat_axis=0, tiled=True), 3, 0
        ),
        jnp.moveaxis(
            lax.all_to_all(value_rows, "view", split_axis=0, concat_axis=0, tiled=True), 3, 0
        ),
    )
    row_peaks, row_totals, row_sums = lax.map(one_head, by_head)
    peak_part = jnp.moveaxis(row_peaks, 0, 3)
    total_part = jnp.moveaxis(row_totals, 0, 3)
    sum_part = jnp.moveaxis(row_sums, 0, 3)
    row_peak = lax.all_to_all(peak_part, "view", split_axis=0, concat_axis=0, tiled=True)
    row_total = lax.all_to_all(total_part, "view", split_axis=0, concat_axis=0, tiled=True)
    row_sum = lax.all_to_all(sum_part, "view", split_axis=0, concat_axis=0, tiled=True)
    row_peak = into_tokens(row_peak, row_blocks, head_groups)
    row_total = into_tokens(row_total, row_blocks, head_groups)
    row_sum = into_tokens(row_sum, row_blocks, head_groups)
    attended = combine((local_peak, local_total, local_sum), (row_peak, row_total, row_sum))
    return attended.reshape(1, ROWS, COLS, HEADS * HS)


PARTS = 4
SKEW = 7
LAG = 2
GROUPS = 2
AHEAD = 2


def pair_kernel(
    req_hbm, q_ref, k_ref, v_ref, o_ref,
    req_ref, queries, kv, outer, inner, crossing, ending, chosen, bias, results, sums, peaks, totals,
    req_sem, load_sem, swap_send, swap_recv, own_send, outer_recv, cross_send, inner_recv, end_send, out_send, out_recv, out_sem,
):
    half, _, _, rows, size = queries.shape
    block = 2 * rows
    span = 4 // PARTS
    me = lax.axis_index("view")
    domain = me % 2
    slot = me // 4
    other = 1 - domain
    twin = me + other - domain
    upper = slot // 2
    end_slot = 3 * upper
    mid_slot = 1 + upper
    is_end = slot == end_slot
    is_mid = slot == mid_slot
    near = me + 4 * (end_slot + mid_slot - 2 * slot)
    across = me + 4 * (3 - 2 * slot)

    def remote(src, dst, send, recv, device):
        return pltpu.make_async_remote_copy(
            src_ref=src, dst_ref=dst, send_sem=send, recv_sem=recv,
            device_id={"view": device}, device_id_type=pl.DeviceIdType.MESH,
        )

    def lanes(at, group):
        return pl.ds(pl.multiple_of((group * half + at) * size, size), size)

    def unit(ref, number):
        return ref.at[pl.ds(number * span, span)]

    def place(at, which, whose):
        return queries.at[at, whose] if which == 2 else kv.at[at * 4 + which * 2 + whose]

    sources = (k_ref, v_ref, q_ref)

    def load(at, which):
        return pltpu.make_async_copy(
            sources[which].at[:, :, lanes(at, domain)], place(at, which, 0), load_sem.at[which, at]
        )

    def swap(at, which):
        return remote(
            sources[which].at[:, :, lanes(at, other)], place(at, which, 1),
            swap_send.at[which], swap_recv.at[which, at], twin,
        )

    def fetched(at, which):
        load(at, which).wait()
        swap(at, which).wait_recv()

    def own_copy(n):
        return remote(unit(kv, n), unit(outer, n), own_send, outer_recv.at[n], near)

    def cross_copy(n):
        return remote(unit(crossing, n), unit(inner, n), cross_send, inner_recv.at[n], across)

    def end_copy(n):
        return remote(unit(ending, n), unit(inner, n), end_send, inner_recv.at[n], near)

    def out_copy(at):
        return remote(results.at[1, at], o_ref.at[:, :, lanes(at, domain)], out_send, out_recv, twin)

    def keep_copy(at):
        return pltpu.make_async_copy(results.at[0, at], o_ref.at[:, :, lanes(at, domain)], out_sem)

    for at in range(AHEAD):
        for which in range(3):
            load(at, which).start()
    request = pltpu.make_async_copy(req_hbm, req_ref, req_sem)
    request.start()
    barrier = pltpu.get_barrier_semaphore()
    for device in (twin, near):
        pl.semaphore_signal(barrier, inc=1, device_id={"view": device}, device_id_type=pl.DeviceIdType.MESH)

    @pl.when(is_mid)
    def _():
        pl.semaphore_signal(barrier, inc=1, device_id={"view": across}, device_id_type=pl.DeviceIdType.MESH)
        pl.semaphore_wait(barrier, 3)

    @pl.when(is_end)
    def _():
        pl.semaphore_wait(barrier, 2)

    for at in range(AHEAD):
        for which in range(2):
            swap(at, which).start()

    def fetch_keys(at):
        @pl.when(at + AHEAD < half)
        def _():
            for which in range(2):
                load(at + AHEAD, which).start()
                swap(at + AHEAD, which).start()

    @pl.when(is_end)
    def _():
        @pl.loop(0, half)
        def _(at):
            for which in range(2):
                load(at, which).wait()
                own_copy(at * PARTS + which * 2).start()
                swap(at, which).wait_recv()
                own_copy(at * PARTS + which * 2 + 1).start()
            fetch_keys(at)

    for at in range(AHEAD):
        swap(at, 2).start()

    request.wait()
    mine = req_ref[slot]
    end_same = (req_ref[end_slot] == mine).astype(jnp.int32)
    mid_same = (req_ref[mid_slot] == mine).astype(jnp.int32)
    far_same = jnp.maximum(
        (req_ref[3 - end_slot] == mine).astype(jnp.int32), (req_ref[3 - mid_slot] == mine).astype(jnp.int32)
    )
    near_same = jnp.minimum(end_same, mid_same)
    paired = jnp.maximum(near_same, far_same)

    query_row = lax.broadcasted_iota(jnp.int32, bias.shape, 0) % rows // COLS
    key_row = lax.broadcasted_iota(jnp.int32, bias.shape, 1) % rows // COLS
    bias[...] = jnp.where(paired > 0, jnp.where(query_row == key_row, 0.0, NEG_FILL), NEG_FILL)

    def pass_across(n):
        @pl.when(is_mid)
        def _():
            own_copy(n).wait_recv()
            at = pl.ds(n * span, span)
            crossing[at] = jnp.where(far_same > 0, kv[at], outer[at])
            cross_copy(n).start()

    def pass_out(n):
        cross_copy(n).wait_recv()

        @pl.when(is_mid)
        def _():
            at = pl.ds(n * span, span)
            ending[at] = jnp.where(near_same > 0, kv[at], inner[at])
            end_copy(n).start()

    scaling = size ** (-0.5) * LOG2E

    def scores_of(keys, asking):
        return (
            lax.dot_general(keys, asking, (((1,), (1,)), ((), ())), preferred_element_type=jnp.float32) * scaling
        )

    def weighted(raised, values):
        return lax.dot_general(
            values, raised.astype(jnp.bfloat16), (((0,), (0,)), ((), ())), preferred_element_type=jnp.float32
        )

    def own_part(at):
        fetched(at, 2)
        scores = scores_of(
            kv[pl.ds(at * 4, 2)].reshape(GROUPS * block, size),
            jnp.concatenate([queries[at, :, group].reshape(block, size) for group in range(GROUPS)], axis=0),
        )
        peak = jnp.max(scores, axis=0, keepdims=True)
        raised = jnp.exp2(scores - peak)
        peaks[at] = peak
        totals[at] = jnp.sum(raised, axis=0, keepdims=True)
        sums[at] = weighted(raised, kv[pl.ds(at * 4 + 2, 2)].reshape(GROUPS * block, size))

    def finish(at):
        @pl.when(is_mid)
        def _():
            chosen[...] = jnp.where(near_same > 0, outer[pl.ds(at * 4, 4)], inner[pl.ds(at * 4, 4)])

        @pl.when(is_end)
        def _():
            chosen[...] = inner[pl.ds(at * 4, 4)]

        for group in range(GROUPS):
            columns = slice(group * block, (group + 1) * block)
            scores = scores_of(
                chosen[0:2, group].reshape(block, size), queries[at, :, group].reshape(block, size)
            ) + bias[...]
            own_peak = peaks[at, :, columns]
            peak = jnp.maximum(own_peak, jnp.max(scores, axis=0, keepdims=True))
            raised = jnp.exp2(scores - peak)
            kept = jnp.exp2(own_peak - peak)
            total = totals[at, :, columns] * kept + jnp.sum(raised, axis=0, keepdims=True)
            summed = sums[at, :, columns] * kept + weighted(raised, chosen[2:4, group].reshape(block, size))
            attended = (summed / total).T.astype(jnp.bfloat16)
            results[:, at, group] = attended.reshape(2, rows, size)
        out_copy(at).start()
        keep_copy(at).start()

    def head(at, first):
        @pl.when(is_mid)
        def _():
            fetch_keys(at)
            for which in range(2):
                fetched(at, which)

        @pl.when(at + AHEAD < half)
        def _():
            load(at + AHEAD, 2).start()
            swap(at + AHEAD, 2).start()

        for part in range(PARTS):
            pass_across(at * PARTS + part)
            if not first or at * PARTS + part >= SKEW:
                pass_out(at * PARTS + part - SKEW)
            if part == 1:
                own_part(at)
            if part == PARTS - 1 and not first:
                finish(at - LAG)

    for at in range(LAG):
        head(at, True)

    @pl.loop(LAG, half)
    def _(at):
        head(at, False)

    for late in range(SKEW):
        number = half * PARTS - SKEW + late
        pass_out(number)
        if (number + 1) % PARTS == 0:
            finish(number // PARTS)

    whole = pl.ds(0, half * size)
    for which in range(3):
        side = sources[which].at[:, :, whole]
        remote(side, side, swap_send.at[which], out_recv, twin).wait_send()

    @pl.when(is_end)
    def _():
        remote(kv, outer, own_send, out_recv, near).wait_send()

    @pl.when(is_mid)
    def _():
        remote(crossing, inner, cross_send, out_recv, across).wait_send()
        remote(ending, inner, end_send, out_recv, near).wait_send()

    pltpu.make_async_copy(results.at[0], results.at[1], out_sem).wait()
    remote(results.at[1], results.at[1], out_send, out_recv, twin).wait()


def pair_shards(query_vectors, key_vectors, value_vectors, request_of_slot):
    rows = ROWS * COLS // GROUPS
    half = HEADS // 2
    flat = [tensor.reshape(GROUPS, rows, HEADS * HS) for tensor in (query_vectors, key_vectors, value_vectors)]
    vmem = pl.BlockSpec(memory_space=pltpu.VMEM)
    hbm = pl.BlockSpec(memory_space=pltpu.HBM)
    bank = pltpu.VMEM((half * 4, GROUPS, rows, HS), jnp.bfloat16)
    line = pltpu.VMEM((half, 1, GROUPS * 2 * rows), jnp.float32)
    one = pltpu.SemaphoreType.DMA
    three = pltpu.SemaphoreType.DMA((3, half))
    units = pltpu.SemaphoreType.DMA((half * PARTS,))
    scores = (2 * ROWS * COLS) ** 2 * half
    out = pl.pallas_call(
        pair_kernel,
        out_shape=jax.ShapeDtypeStruct((GROUPS, rows, HEADS * HS), jnp.bfloat16),
        in_specs=[hbm, hbm, hbm, hbm],
        out_specs=vmem,
        scratch_shapes=[
            pltpu.SMEM(request_of_slot.shape, jnp.int32),
            pltpu.VMEM((half, 2, GROUPS, rows, HS), jnp.bfloat16),
            bank, bank, bank, bank, bank,
            pltpu.VMEM((4, GROUPS, rows, HS), jnp.bfloat16),
            pltpu.VMEM((2 * rows, 2 * rows), jnp.float32),
            pltpu.VMEM((2, half, GROUPS, rows, HS), jnp.bfloat16),
            pltpu.VMEM((half, HS, GROUPS * 2 * rows), jnp.float32),
            line, line,
            one, three, pltpu.SemaphoreType.DMA((3,)), three, one, units, one, units, one, one, one, one,
        ],
        compiler_params=pltpu.CompilerParams(
            collective_id=0, has_side_effects=True, vmem_limit_bytes=VMEM_LIMIT
        ),
        cost_estimate=pl.CostEstimate(
            flops=6 * scores * HS, bytes_accessed=8 * ROWS * COLS * HEADS * HS, transcendentals=2 * scores
        ),
    )(request_of_slot, *flat)
    return out.reshape(1, ROWS, COLS, HEADS * HS)


def solution(mesh):
    slot_count = mesh.shape["view"] // 4
    shards = pair_shards if slot_count == 4 else general_shards
    return jax.shard_map(
        shards,
        mesh=mesh,
        in_specs=(
            P(("groups", "view"), None, None, None),
            P(("groups", "view"), None, None, None),
            P(("groups", "view"), None, None, None),
            P("groups"),
        ),
        out_specs=P(("groups", "view"), None, None, None),
        check_vma=False,
    )
```

profile of v0, /device:TPU:0, one launch (start us, length us, event | category | flops | bytes accessed | tf_op | source)
XLA Modules:
  0.0 63.4 jit_solution(14198875025684612171)
XLA Ops:
  0.0 0.0 copy-start
  0.0 0.7 %copy-done = s32[4]{0:T(128)S(1)} copy-done((s32[4]{0:T(128)S(1)}, s32[4]{0:T(128)}, u32[]{:S(2)}) %copy-start) | copy-done | bytes 40
  0.7 61.8 %shard_map.46 = bf16[2,64,4096]{2,1,0:T(8,128)(2,1)S(1)} custom-call(s32[4]{0:T(128)S(1)} %copy-done, bf16[2,64,4096]{2,1,0:T(8,128)(2,1)} %bitcast.5, bf16[2,64,4096]{2,1,0:T(8,128)(2,1)} %bitcast.6, bf16[2,64,4096]{2,1,0:T(8,128)(2,1)} %bitcast.7), custom_call_target="tpu_custom_call" | custom-call | flops 805306368 | bytes 4194304 | tf_op jit(solution)/shard_map/pallas_call | solution.py:442
  62.4 1.0 %copy.6 = bf16[1,16,8,4096]{3,2,1,0:T(8,128)(2,1)} copy(bf16[1,16,8,4096]{3,2,1,0:T(8,128)(2,1)S(1)} %bitcast.4) | data formatting | bytes 2097152
Async XLA Ops:
  0.0 0.7 %copy-start = (s32[4]{0:T(128)S(1)}, s32[4]{0:T(128)}, u32[]{:S(2)}) copy-start(s32[4]{0:T(128)} %req_hbm.1) | copy-start | bytes 52
where the time goes:
time: 64 us; the launch traced here: 63.4 us
  Pallas kernels  61.8 us (97%)
  local copies, waits for them, and re-layouts  1.63 us (3%)
    pallas_call x1, Pallas kernels, pair_shards(): pl.pallas_call(pair_kernel, out_shape=jax.ShapeDtypeStruct((GROUPS, rows,...  61.8 us
    unnamed x3, local copies, waits for them, and re-layouts  1.63 us

commit v1 on v0

--- a/solution.py
+++ b/solution.py
@@ -178,10 +178,10 @@
 
 
 PARTS = 4
-SKEW = 7
+SKEW = 5
+CHUNK = 4
 LAG = 2
 GROUPS = 2
-AHEAD = 2
 
 
 def pair_kernel(
@@ -189,9 +189,10 @@
     req_ref, queries, kv, outer, inner, crossing, ending, chosen, bias, results, sums, peaks, totals,
     req_sem, load_sem, swap_send, swap_recv, own_send, outer_recv, cross_send, inner_recv, end_send, out_send, out_recv, out_sem,
 ):
-    half, _, _, rows, size = queries.shape
+    half, size, _ = sums.shape
+    rows = queries.shape[2]
     block = 2 * rows
-    span = 4 // PARTS
+    chunks = half // CHUNK
     me = lax.axis_index("view")
     domain = me % 2
     slot = me // 4
@@ -214,37 +215,37 @@
     def lanes(at, group):
         return pl.ds(pl.multiple_of((group * half + at) * size, size), size)
 
-    def unit(ref, number):
-        return ref.at[pl.ds(number * span, span)]
-
-    def place(at, which, whose):
-        return queries.at[at, whose] if which == 2 else kv.at[at * 4 + which * 2 + whose]
-
     sources = (k_ref, v_ref, q_ref)
 
-    def load(at, which):
+    def wide(chunk, group):
+        return pl.ds(pl.multiple_of((group * half + chunk * CHUNK) * size, CHUNK * size), CHUNK * size)
+
+    def place(chunk, which, whose):
+        columns = wide(chunk, 0)
+        return queries.at[whose, :, :, columns] if which == 2 else kv.at[which, whose, :, :, columns]
+
+    def load(chunk, which):
         return pltpu.make_async_copy(
-            sources[which].at[:, :, lanes(at, domain)], place(at, which, 0), load_sem.at[which, at]
-        )
-
-    def swap(at, which):
+            sources[which].at[:, :, wide(chunk, domain)], place(chunk, which, 0), load_sem.at[which, chunk]
+        )
+
+    def swap(chunk, which):
         return remote(
-            sources[which].at[:, :, lanes(at, other)], place(at, which, 1),
-            swap_send.at[which], swap_recv.at[which, at], twin,
-        )
-
-    def fetched(at, which):
-        load(at, which).wait()
-        swap(at, which).wait_recv()
-
-    def own_copy(n):
-        return remote(unit(kv, n), unit(outer, n), own_send, outer_recv.at[n], near)
+            sources[which].at[:, :, wide(chunk, other)], place(chunk, which, 1),
+            swap_send.at[which], swap_recv.at[which, chunk], twin,
+        )
+
+    def own_copy(at, part):
+        n = at * PARTS + part
+        return remote(
+            kv.at[part // 2, part % 2, :, :, lanes(at, 0)], outer.at[n], own_send, outer_recv.at[n], near
+        )
 
     def cross_copy(n):
-        return remote(unit(crossing, n), unit(inner, n), cross_send, inner_recv.at[n], across)
+        return remote(crossing.at[n], inner.at[n], cross_send, inner_recv.at[n], across)
 
     def end_copy(n):
-        return remote(unit(ending, n), unit(inner, n), end_send, inner_recv.at[n], near)
+        return remote(ending.at[n], inner.at[n], end_send, inner_recv.at[n], near)
 
     def out_copy(at):
         return remote(results.at[1, at], o_ref.at[:, :, lanes(at, domain)], out_send, out_recv, twin)
@@ -252,9 +253,6 @@
     def keep_copy(at):
         return pltpu.make_async_copy(results.at[0, at], o_ref.at[:, :, lanes(at, domain)], out_sem)
 
-    for at in range(AHEAD):
-        for which in range(3):
-            load(at, which).start()
     request = pltpu.make_async_copy(req_hbm, req_ref, req_sem)
     request.start()
     barrier = pltpu.get_barrier_semaphore()
@@ -264,36 +262,37 @@
     @pl.when(is_mid)
     def _():
         pl.semaphore_signal(barrier, inc=1, device_id={"view": across}, device_id_type=pl.DeviceIdType.MESH)
+
+    for chunk in range(chunks):
+        for which in range(3):
+            load(chunk, which).start()
+
+    @pl.when(is_mid)
+    def _():
         pl.semaphore_wait(barrier, 3)
 
     @pl.when(is_end)
     def _():
         pl.semaphore_wait(barrier, 2)
 
-    for at in range(AHEAD):
-        for which in range(2):
-            swap(at, which).start()
-
-    def fetch_keys(at):
-        @pl.when(at + AHEAD < half)
-        def _():
-            for which in range(2):
-                load(at + AHEAD, which).start()
-                swap(at + AHEAD, which).start()
+    for chunk in range(chunks):
+        for which in range(3):
+            swap(chunk, which).start()
+
+    def fetched(at, which):
+        @pl.when(at % CHUNK == 0)
+        def _():
+            load(at // CHUNK, which).wait()
+            swap(at // CHUNK, which).wait_recv()
 
     @pl.when(is_end)
     def _():
         @pl.loop(0, half)
         def _(at):
             for which in range(2):
-                load(at, which).wait()
-                own_copy(at * PARTS + which * 2).start()
-                swap(at, which).wait_recv()
-                own_copy(at * PARTS + which * 2 + 1).start()
-            fetch_keys(at)
-
-    for at in range(AHEAD):
-        swap(at, 2).start()
+                fetched(at, which)
+                for whose in range(2):
+                    own_copy(at, which * 2 + whose).start()
 
     request.wait()
     mine = req_ref[slot]
@@ -309,21 +308,24 @@
     key_row = lax.broadcasted_iota(jnp.int32, bias.shape, 1) % rows // COLS
     bias[...] = jnp.where(paired > 0, jnp.where(query_row == key_row, 0.0, NEG_FILL), NEG_FILL)
 
-    def pass_across(n):
+    def own_unit(at, part):
+        return kv[part // 2, part % 2, :, :, lanes(at, 0)]
+
+    def pass_across(at, part):
         @pl.when(is_mid)
         def _():
-            own_copy(n).wait_recv()
-            at = pl.ds(n * span, span)
-            crossing[at] = jnp.where(far_same > 0, kv[at], outer[at])
+            n = at * PARTS + part
+            own_copy(at, part).wait_recv()
+            crossing[n] = jnp.where(far_same > 0, own_unit(at, part), outer[n])
             cross_copy(n).start()
 
-    def pass_out(n):
+    def pass_out(at, part):
+        n = at * PARTS + part
         cross_copy(n).wait_recv()
 
         @pl.when(is_mid)
         def _():
-            at = pl.ds(n * span, span)
-            ending[at] = jnp.where(near_same > 0, kv[at], inner[at])
+            ending[n] = jnp.where(near_same > 0, own_unit(at, part), inner[n])
             end_copy(n).start()
 
     scaling = size ** (-0.5) * LOG2E
@@ -339,16 +341,16 @@
         )
 
     def own_part(at):
-        fetched(at, 2)
+        asking = queries[:, :, :, lanes(at, 0)]
         scores = scores_of(
-            kv[pl.ds(at * 4, 2)].reshape(GROUPS * block, size),
-            jnp.concatenate([queries[at, :, group].reshape(block, size) for group in range(GROUPS)], axis=0),
+            kv[0, :, :, :, lanes(at, 0)].reshape(GROUPS * block, size),
+            jnp.concatenate([asking[:, group].reshape(block, size) for group in range(GROUPS)], axis=0),
         )
         peak = jnp.max(scores, axis=0, keepdims=True)
         raised = jnp.exp2(scores - peak)
         peaks[at] = peak
         totals[at] = jnp.sum(raised, axis=0, keepdims=True)
-        sums[at] = weighted(raised, kv[pl.ds(at * 4 + 2, 2)].reshape(GROUPS * block, size))
+        sums[at] = weighted(raised, kv[1, :, :, :, lanes(at, 0)].reshape(GROUPS * block, size))
 
     def finish(at):
         @pl.when(is_mid)
@@ -362,7 +364,7 @@
         for group in range(GROUPS):
             columns = slice(group * block, (group + 1) * block)
             scores = scores_of(
-                chosen[0:2, group].reshape(block, size), queries[at, :, group].reshape(block, size)
+                chosen[0:2, group].reshape(block, size), queries[:, group, :, lanes(at, 0)].reshape(block, size)
             ) + bias[...]
             own_peak = peaks[at, :, columns]
             peak = jnp.maximum(own_peak, jnp.max(scores, axis=0, keepdims=True))
@@ -378,19 +380,15 @@
     def head(at, first):
         @pl.when(is_mid)
         def _():
-            fetch_keys(at)
             for which in range(2):
                 fetched(at, which)
 
-        @pl.when(at + AHEAD < half)
-        def _():
-            load(at + AHEAD, 2).start()
-            swap(at + AHEAD, 2).start()
-
+        fetched(at, 2)
         for part in range(PARTS):
-            pass_across(at * PARTS + part)
-            if not first or at * PARTS + part >= SKEW:
-                pass_out(at * PARTS + part - SKEW)
+            pass_across(at, part)
+            behind = part - SKEW
+            if not first or at * PARTS + behind >= 0:
+                pass_out(at + behind // PARTS, behind % PARTS)
             if part == 1:
                 own_part(at)
             if part == PARTS - 1 and not first:
@@ -403,10 +401,9 @@
     def _(at):
         head(at, False)
 
-    for late in range(SKEW):
-        number = half * PARTS - SKEW + late
-        pass_out(number)
-        if (number + 1) % PARTS == 0:
+    for number in range(half * PARTS - SKEW, half * PARTS):
+        pass_out(number // PARTS, number % PARTS)
+        if number % PARTS == PARTS - 1:
             finish(number // PARTS)
 
     whole = pl.ds(0, half * size)
@@ -416,7 +413,7 @@
 
     @pl.when(is_end)
     def _():
-        remote(kv, outer, own_send, out_recv, near).wait_send()
+        remote(outer, outer, own_send, out_recv, near).wait_send()
 
     @pl.when(is_mid)
     def _():
@@ -436,7 +433,7 @@
     bank = pltpu.VMEM((half * 4, GROUPS, rows, HS), jnp.bfloat16)
     line = pltpu.VMEM((half, 1, GROUPS * 2 * rows), jnp.float32)
     one = pltpu.SemaphoreType.DMA
-    three = pltpu.SemaphoreType.DMA((3, half))
+    three = pltpu.SemaphoreType.DMA((3, half // CHUNK))
     units = pltpu.SemaphoreType.DMA((half * PARTS,))
     scores = (2 * ROWS * COLS) ** 2 * half
     out = pl.pallas_call(
@@ -446,8 +443,9 @@
         out_specs=vmem,
         scratch_shapes=[
             pltpu.SMEM(request_of_slot.shape, jnp.int32),
-            pltpu.VMEM((half, 2, GROUPS, rows, HS), jnp.bfloat16),
-            bank, bank, bank, bank, bank,
+            pltpu.VMEM((2, GROUPS, rows, half * HS), jnp.bfloat16),
+            pltpu.VMEM((2, 2, GROUPS, rows, half * HS), jnp.bfloat16),
+            bank, bank, bank, bank,
             pltpu.VMEM((4, GROUPS, rows, HS), jnp.bfloat16),
             pltpu.VMEM((2 * rows, 2 * rows), jnp.float32),
             pltpu.VMEM((2, half, GROUPS, rows, HS), jnp.bfloat16),

time: 64 us -> 62.7 us (0.980)
  Pallas kernels: 61.8 us -> 60.9 us
    pallas_call x1, Pallas kernels: 61.8 us -> 60.9 us  [pair_shards(): pl.pallas_call(pair_kernel, out_shape=jax.ShapeDtypeStruct((GROUPS, rows,...]
where the time goes in v1:
time: 62.7 us; the launch traced here: 62.5 us
  Pallas kernels  60.9 us (97%)
  local copies, waits for them, and re-layouts  1.63 us (3%)
    pallas_call x1, Pallas kernels, pair_shards(): pl.pallas_call(pair_kernel, out_shape=jax.ShapeDtypeStruct((GROUPS, rows,...  60.9 us
    unnamed x3, local copies, waits for them, and re-layouts  1.63 us

profile of v1, /device:TPU:0, one launch (start us, length us, event | category | flops | bytes accessed | tf_op | source)
XLA Modules:
  0.0 62.5 jit_solution(4727468505593980543)
XLA Ops:
  0.0 0.0 copy-start
  0.0 0.7 %copy-done = s32[4]{0:T(128)S(1)} copy-done((s32[4]{0:T(128)S(1)}, s32[4]{0:T(128)}, u32[]{:S(2)}) %copy-start) | copy-done | bytes 40
  0.7 60.9 %shard_map.46 = bf16[2,64,4096]{2,1,0:T(8,128)(2,1)S(1)} custom-call(s32[4]{0:T(128)S(1)} %copy-done, bf16[2,64,4096]{2,1,0:T(8,128)(2,1)} %bitcast.5, bf16[2,64,4096]{2,1,0:T(8,128)(2,1)} %bitcast.6, bf16[2,64,4096]{2,1,0:T(8,128)(2,1)} %bitcast.7), custom_call_target="tpu_custom_call" | custom-call | flops 805306368 | bytes 4194304 | tf_op jit(solution)/shard_map/pallas_call | solution.py:439
  61.6 1.0 %copy.6 = bf16[1,16,8,4096]{3,2,1,0:T(8,128)(2,1)} copy(bf16[1,16,8,4096]{3,2,1,0:T(8,128)(2,1)S(1)} %bitcast.4) | data formatting | bytes 2097152
Async XLA Ops:
  0.0 0.7 %copy-start = (s32[4]{0:T(128)S(1)}, s32[4]{0:T(128)}, u32[]{:S(2)}) copy-start(s32[4]{0:T(128)} %req_hbm.1) | copy-start | bytes 52

commit v2 on v1

--- a/solution.py
+++ b/solution.py
@@ -238,7 +238,7 @@
     def own_copy(at, part):
         n = at * PARTS + part
         return remote(
-            kv.at[part // 2, part % 2, :, :, lanes(at, 0)], outer.at[n], own_send, outer_recv.at[n], near
+            kv.at[part % 2, part // 2, :, :, lanes(at, 0)], outer.at[n], own_send, outer_recv.at[n], near
         )
 
     def cross_copy(n):
@@ -275,7 +275,17 @@
     def _():
         pl.semaphore_wait(barrier, 2)
 
-    for chunk in range(chunks):
+    for which in range(2):
+        swap(0, which).start()
+
+    @pl.when(is_end)
+    def _():
+        for which in range(2):
+            load(0, which).wait()
+            own_copy(0, which).start()
+
+    swap(0, 2).start()
+    for chunk in range(1, chunks):
         for which in range(3):
             swap(chunk, which).start()
 
@@ -287,12 +297,16 @@
 
     @pl.when(is_end)
     def _():
-        @pl.loop(0, half)
+        for which in range(2):
+            swap(0, which).wait_recv()
+            own_copy(0, 2 + which).start()
+
+        @pl.loop(1, half)
         def _(at):
             for which in range(2):
                 fetched(at, which)
-                for whose in range(2):
-                    own_copy(at, which * 2 + whose).start()
+            for part in range(PARTS):
+                own_copy(at, part).start()
 
     request.wait()
     mine = req_ref[slot]
@@ -309,7 +323,7 @@
     bias[...] = jnp.where(paired > 0, jnp.where(query_row == key_row, 0.0, NEG_FILL), NEG_FILL)
 
     def own_unit(at, part):
-        return kv[part // 2, part % 2, :, :, lanes(at, 0)]
+        return kv[part % 2, part // 2, :, :, lanes(at, 0)]
 
     def pass_across(at, part):
         @pl.when(is_mid)
@@ -361,17 +375,20 @@
         def _():
             chosen[...] = inner[pl.ds(at * 4, 4)]
 
+        def both(which, group):
+            return jnp.concatenate([chosen[which, group], chosen[2 + which, group]], axis=0)
+
         for group in range(GROUPS):
             columns = slice(group * block, (group + 1) * block)
             scores = scores_of(
-                chosen[0:2, group].reshape(block, size), queries[:, group, :, lanes(at, 0)].reshape(block, size)
+                both(0, group), queries[:, group, :, lanes(at, 0)].reshape(block, size)
             ) + bias[...]
             own_peak = peaks[at, :, columns]
             peak = jnp.maximum(own_peak, jnp.max(scores, axis=0, keepdims=True))
             raised = jnp.exp2(scores - peak)
             kept = jnp.exp2(own_peak - peak)
             total = totals[at, :, columns] * kept + jnp.sum(raised, axis=0, keepdims=True)
-            summed = sums[at, :, columns] * kept + weighted(raised, chosen[2:4, group].reshape(block, size))
+            summed = sums[at, :, columns] * kept + weighted(raised, both(1, group))
             attended = (summed / total).T.astype(jnp.bfloat16)
             results[:, at, group] = attended.reshape(2, rows, size)
         out_copy(at).start()

time: 62.7 us -> 61.6 us (0.982)
  Pallas kernels: 60.9 us -> 59.8 us
    pallas_call x1, Pallas kernels: 60.9 us -> 59.8 us  [pair_shards(): pl.pallas_call(pair_kernel, out_shape=jax.ShapeDtypeStruct((GROUPS, rows,...]
where the time goes in v2:
time: 61.6 us; the launch traced here: 61.5 us
  Pallas kernels  59.8 us (97%)
  local copies, waits for them, and re-layouts  1.63 us (3%)
    pallas_call x1, Pallas kernels, pair_shards(): pl.pallas_call(pair_kernel, out_shape=jax.ShapeDtypeStruct((GROUPS, rows,...  59.8 us
    unnamed x3, local copies, waits for them, and re-layouts  1.63 us

profile of v2, /device:TPU:0, one launch (start us, length us, event | category | flops | bytes accessed | tf_op | source)
XLA Modules:
  0.0 61.5 jit_solution(12798443572420692657)
XLA Ops:
  0.0 0.0 copy-start
  0.0 0.7 %copy-done = s32[4]{0:T(128)S(1)} copy-done((s32[4]{0:T(128)S(1)}, s32[4]{0:T(128)}, u32[]{:S(2)}) %copy-start) | copy-done | bytes 40
  0.7 59.8 %shard_map.46 = bf16[2,64,4096]{2,1,0:T(8,128)(2,1)S(1)} custom-call(s32[4]{0:T(128)S(1)} %copy-done, bf16[2,64,4096]{2,1,0:T(8,128)(2,1)} %bitcast.5, bf16[2,64,4096]{2,1,0:T(8,128)(2,1)} %bitcast.6, bf16[2,64,4096]{2,1,0:T(8,128)(2,1)} %bitcast.7), custom_call_target="tpu_custom_call" | custom-call | flops 805306368 | bytes 4194304 | tf_op jit(solution)/shard_map/pallas_call | solution.py:456
  60.5 1.0 %copy.6 = bf16[1,16,8,4096]{3,2,1,0:T(8,128)(2,1)} copy(bf16[1,16,8,4096]{3,2,1,0:T(8,128)(2,1)S(1)} %bitcast.4) | data formatting | bytes 2097152
Async XLA Ops:
  0.0 0.7 %copy-start = (s32[4]{0:T(128)S(1)}, s32[4]{0:T(128)}, u32[]{:S(2)}) copy-start(s32[4]{0:T(128)} %req_hbm.1) | copy-start | bytes 52

commit v3 on v2

--- a/solution.py
+++ b/solution.py
@@ -178,9 +178,9 @@
 
 
 PARTS = 4
-SKEW = 5
+SKEW = 4
 CHUNK = 4
-LAG = 2
+LAG = 1
 GROUPS = 2
 
 
@@ -362,11 +362,10 @@
         )
         peak = jnp.max(scores, axis=0, keepdims=True)
         raised = jnp.exp2(scores - peak)
-        peaks[at] = peak
-        totals[at] = jnp.sum(raised, axis=0, keepdims=True)
-        sums[at] = weighted(raised, kv[1, :, :, :, lanes(at, 0)].reshape(GROUPS * block, size))
-
-    def finish(at):
+        total = jnp.sum(raised, axis=0, keepdims=True)
+        return peak, total, weighted(raised, kv[1, :, :, :, lanes(at, 0)].reshape(GROUPS * block, size))
+
+    def choose(at):
         @pl.when(is_mid)
         def _():
             chosen[...] = jnp.where(near_same > 0, outer[pl.ds(at * 4, 4)], inner[pl.ds(at * 4, 4)])
@@ -375,24 +374,37 @@
         def _():
             chosen[...] = inner[pl.ds(at * 4, 4)]
 
+    def pair_part(at):
         def both(which, group):
             return jnp.concatenate([chosen[which, group], chosen[2 + which, group]], axis=0)
 
+        attended = []
         for group in range(GROUPS):
             columns = slice(group * block, (group + 1) * block)
-            scores = scores_of(
-                both(0, group), queries[:, group, :, lanes(at, 0)].reshape(block, size)
-            ) + bias[...]
+            scores = scores_of(both(0, group), queries[:, group, :, lanes(at, 0)].reshape(block, size)) + bias[...]
             own_peak = peaks[at, :, columns]
             peak = jnp.maximum(own_peak, jnp.max(scores, axis=0, keepdims=True))
             raised = jnp.exp2(scores - peak)
             kept = jnp.exp2(own_peak - peak)
             total = totals[at, :, columns] * kept + jnp.sum(raised, axis=0, keepdims=True)
             summed = sums[at, :, columns] * kept + weighted(raised, both(1, group))
-            attended = (summed / total).T.astype(jnp.bfloat16)
-            results[:, at, group] = attended.reshape(2, rows, size)
-        out_copy(at).start()
-        keep_copy(at).start()
+            attended.append((summed * (1.0 / total)).T.astype(jnp.bfloat16).reshape(2, rows, size))
+        return attended
+
+    def compute(own, done):
+        if done is not None:
+            choose(done)
+            attended = pair_part(done)
+        if own is not None:
+            peaks_own, totals_own, sums_own = own_part(own)
+            peaks[own] = peaks_own
+            totals[own] = totals_own
+            sums[own] = sums_own
+        if done is not None:
+            for group in range(GROUPS):
+                results[:, done, group] = attended[group]
+            out_copy(done).start()
+            keep_copy(done).start()
 
     def head(at, first):
         @pl.when(is_mid)
@@ -406,10 +418,8 @@
             behind = part - SKEW
             if not first or at * PARTS + behind >= 0:
                 pass_out(at + behind // PARTS, behind % PARTS)
-            if part == 1:
-                own_part(at)
-            if part == PARTS - 1 and not first:
-                finish(at - LAG)
+            if part == PARTS - 1:
+                compute(at, None if first else at - LAG)
 
     for at in range(LAG):
         head(at, True)
@@ -421,7 +431,7 @@
     for number in range(half * PARTS - SKEW, half * PARTS):
         pass_out(number // PARTS, number % PARTS)
         if number % PARTS == PARTS - 1:
-            finish(number // PARTS)
+            compute(None, number // PARTS)
 
     whole = pl.ds(0, half * size)
     for which in range(3):

time: 61.6 us -> 61.5 us (level)
  no operation moved by 1% of the time
where the time goes in v3:
time: 61.5 us; the launch traced here: 61.4 us
  Pallas kernels  59.7 us (97%)
  local copies, waits for them, and re-layouts  1.63 us (3%)
    pallas_call x1, Pallas kernels, pair_shards(): pl.pallas_call(pair_kernel, out_shape=jax.ShapeDtypeStruct((GROUPS, rows,...  59.7 us
    unnamed x3, local copies, waits for them, and re-layouts  1.63 us

profile of v3, /device:TPU:0, one launch (start us, length us, event | category | flops | bytes accessed | tf_op | source)
XLA Modules:
  0.0 61.4 jit_solution(12007768403461693501)
XLA Ops:
  0.0 0.0 copy-start
  0.0 0.7 %copy-done = s32[4]{0:T(128)S(1)} copy-done((s32[4]{0:T(128)S(1)}, s32[4]{0:T(128)}, u32[]{:S(2)}) %copy-start) | copy-done | bytes 40
  0.7 59.7 %shard_map.46 = bf16[2,64,4096]{2,1,0:T(8,128)(2,1)S(1)} custom-call(s32[4]{0:T(128)S(1)} %copy-done, bf16[2,64,4096]{2,1,0:T(8,128)(2,1)} %bitcast.5, bf16[2,64,4096]{2,1,0:T(8,128)(2,1)} %bitcast.6, bf16[2,64,4096]{2,1,0:T(8,128)(2,1)} %bitcast.7), custom_call_target="tpu_custom_call" | custom-call | flops 805306368 | bytes 4194304 | tf_op jit(solution)/shard_map/pallas_call | solution.py:466
  60.4 1.0 %copy.6 = bf16[1,16,8,4096]{3,2,1,0:T(8,128)(2,1)} copy(bf16[1,16,8,4096]{3,2,1,0:T(8,128)(2,1)S(1)} %bitcast.4) | data formatting | bytes 2097152
Async XLA Ops:
  0.0 0.7 %copy-start = (s32[4]{0:T(128)S(1)}, s32[4]{0:T(128)}, u32[]{:S(2)}) copy-start(s32[4]{0:T(128)} %req_hbm.1) | copy-start | bytes 52

commit v4 on v3

--- a/solution.py
+++ b/solution.py
@@ -178,9 +178,9 @@
 
 
 PARTS = 4
-SKEW = 4
+SKEW = 6
 CHUNK = 4
-LAG = 1
+LAG = 2
 GROUPS = 2
 
 

time: 61.5 us -> 62 us (level)
  no operation moved by 1% of the time
where the time goes in v4:
time: 62 us; the launch traced here: 61.8 us
  Pallas kernels  60.2 us (97%)
  local copies, waits for them, and re-layouts  1.63 us (3%)
    pallas_call x1, Pallas kernels, pair_shards(): pl.pallas_call(pair_kernel, out_shape=jax.ShapeDtypeStruct((GROUPS, rows,...  60.2 us
    unnamed x3, local copies, waits for them, and re-layouts  1.63 us

profile of v4, /device:TPU:0, one launch (start us, length us, event | category | flops | bytes accessed | tf_op | source)
XLA Modules:
  0.0 61.8 jit_solution(2293455762175235414)
XLA Ops:
  0.0 0.0 copy-start
  0.0 0.7 %copy-done = s32[4]{0:T(128)S(1)} copy-done((s32[4]{0:T(128)S(1)}, s32[4]{0:T(128)}, u32[]{:S(2)}) %copy-start) | copy-done | bytes 40
  0.7 60.2 %shard_map.46 = bf16[2,64,4096]{2,1,0:T(8,128)(2,1)S(1)} custom-call(s32[4]{0:T(128)S(1)} %copy-done, bf16[2,64,4096]{2,1,0:T(8,128)(2,1)} %bitcast.5, bf16[2,64,4096]{2,1,0:T(8,128)(2,1)} %bitcast.6, bf16[2,64,4096]{2,1,0:T(8,128)(2,1)} %bitcast.7), custom_call_target="tpu_custom_call" | custom-call | flops 805306368 | bytes 4194304 | tf_op jit(solution)/shard_map/pallas_call | solution.py:466
  60.9 1.0 %copy.6 = bf16[1,16,8,4096]{3,2,1,0:T(8,128)(2,1)} copy(bf16[1,16,8,4096]{3,2,1,0:T(8,128)(2,1)S(1)} %bitcast.4) | data formatting | bytes 2097152
Async XLA Ops:
  0.0 0.7 %copy-start = (s32[4]{0:T(128)S(1)}, s32[4]{0:T(128)}, u32[]{:S(2)}) copy-start(s32[4]{0:T(128)} %req_hbm.1) | copy-start | bytes 52

commit v5 on v3

--- a/solution.py
+++ b/solution.py
@@ -285,9 +285,12 @@
             own_copy(0, which).start()
 
     swap(0, 2).start()
-    for chunk in range(1, chunks):
-        for which in range(3):
-            swap(chunk, which).start()
+
+    def exchange_next(at):
+        @pl.when((at % CHUNK == CHUNK // 2) & (at < half - CHUNK))
+        def _():
+            for which in range(3):
+                swap(at // CHUNK + 1, which).start()
 
     def fetched(at, which):
         @pl.when(at % CHUNK == 0)
@@ -307,6 +310,7 @@
                 fetched(at, which)
             for part in range(PARTS):
                 own_copy(at, part).start()
+            exchange_next(at)
 
     request.wait()
     mine = req_ref[slot]
@@ -409,6 +413,7 @@
     def head(at, first):
         @pl.when(is_mid)
         def _():
+            exchange_next(at)
             for which in range(2):
                 fetched(at, which)
 

time: 61.5 us -> 61.5 us (level)
  no operation moved by 1% of the time
where the time goes in v5:
time: 61.5 us; the launch traced here: 61.4 us
  Pallas kernels  59.7 us (97%)
  local copies, waits for them, and re-layouts  1.63 us (3%)
    pallas_call x1, Pallas kernels, pair_shards(): pl.pallas_call(pair_kernel, out_shape=jax.ShapeDtypeStruct((GROUPS, rows,...  59.7 us
    unnamed x3, local copies, waits for them, and re-layouts  1.63 us

profile of v5, /device:TPU:0, one launch (start us, length us, event | category | flops | bytes accessed | tf_op | source)
XLA Modules:
  0.0 61.4 jit_solution(438396409210417559)
XLA Ops:
  0.0 0.0 copy-start
  0.0 0.7 %copy-done = s32[4]{0:T(128)S(1)} copy-done((s32[4]{0:T(128)S(1)}, s32[4]{0:T(128)}, u32[]{:S(2)}) %copy-start) | copy-done | bytes 40
  0.7 59.7 %shard_map.46 = bf16[2,64,4096]{2,1,0:T(8,128)(2,1)S(1)} custom-call(s32[4]{0:T(128)S(1)} %copy-done, bf16[2,64,4096]{2,1,0:T(8,128)(2,1)} %bitcast.5, bf16[2,64,4096]{2,1,0:T(8,128)(2,1)} %bitcast.6, bf16[2,64,4096]{2,1,0:T(8,128)(2,1)} %bitcast.7), custom_call_target="tpu_custom_call" | custom-call | flops 805306368 | bytes 4194304 | tf_op jit(solution)/shard_map/pallas_call | solution.py:471
  60.4 1.0 %copy.6 = bf16[1,16,8,4096]{3,2,1,0:T(8,128)(2,1)} copy(bf16[1,16,8,4096]{3,2,1,0:T(8,128)(2,1)S(1)} %bitcast.4) | data formatting | bytes 2097152
Async XLA Ops:
  0.0 0.7 %copy-start = (s32[4]{0:T(128)S(1)}, s32[4]{0:T(128)}, u32[]{:S(2)}) copy-start(s32[4]{0:T(128)} %req_hbm.1) | copy-start | bytes 52

commit v6 on v5

--- a/solution.py
+++ b/solution.py
@@ -178,9 +178,9 @@
 
 
 PARTS = 4
-SKEW = 4
+SKEW = 5
 CHUNK = 4
-LAG = 1
+LAG = 2
 GROUPS = 2
 
 

time: 61.5 us -> 61.7 us (level)
  no operation moved by 1% of the time
where the time goes in v6:
time: 61.7 us; the launch traced here: 61.5 us
  Pallas kernels  59.9 us (97%)
  local copies, waits for them, and re-layouts  1.63 us (3%)
    pallas_call x1, Pallas kernels, pair_shards(): pl.pallas_call(pair_kernel, out_shape=jax.ShapeDtypeStruct((GROUPS, rows,...  59.9 us
    unnamed x3, local copies, waits for them, and re-layouts  1.63 us

profile of v6, /device:TPU:0, one launch (start us, length us, event | category | flops | bytes accessed | tf_op | source)
XLA Modules:
  0.0 61.5 jit_solution(939734891781140008)
XLA Ops:
  0.0 0.0 copy-start
  0.0 0.7 %copy-done = s32[4]{0:T(128)S(1)} copy-done((s32[4]{0:T(128)S(1)}, s32[4]{0:T(128)}, u32[]{:S(2)}) %copy-start) | copy-done | bytes 40
  0.7 59.9 %shard_map.46 = bf16[2,64,4096]{2,1,0:T(8,128)(2,1)S(1)} custom-call(s32[4]{0:T(128)S(1)} %copy-done, bf16[2,64,4096]{2,1,0:T(8,128)(2,1)} %bitcast.5, bf16[2,64,4096]{2,1,0:T(8,128)(2,1)} %bitcast.6, bf16[2,64,4096]{2,1,0:T(8,128)(2,1)} %bitcast.7), custom_call_target="tpu_custom_call" | custom-call | flops 805306368 | bytes 4194304 | tf_op jit(solution)/shard_map/pallas_call | solution.py:471
  60.5 1.0 %copy.6 = bf16[1,16,8,4096]{3,2,1,0:T(8,128)(2,1)} copy(bf16[1,16,8,4096]{3,2,1,0:T(8,128)(2,1)S(1)} %bitcast.4) | data formatting | bytes 2097152
Async XLA Ops:
  0.0 0.7 %copy-start = (s32[4]{0:T(128)S(1)}, s32[4]{0:T(128)}, u32[]{:S(2)}) copy-start(s32[4]{0:T(128)} %req_hbm.1) | copy-start | bytes 52
